TPU v7x, 256 devices: a whole 4x4x8 slice. The times are simulated.
256 devices in a mesh: sec: 16 (over z, core), op: 16 (over x, y).
Axes of the slice: x: 4, y: 4, z: 8, core: 2. Of those that a mesh axis runs over, the one named last changes fastest.
Arguments:
- theta: float32 [32, 512, 512], P('sec', 'op'), may hold values from -6 to 6
- counts: int32 [32], P('sec'), may hold values from 256 to 512, as said below
- pair_source: int32 [256], P('sec'), may hold values from 0 to 1
- pair_target: int32 [256], P('sec'), may hold values from 0 to 31
- left_ops: float32 [1024, 512, 512], P(('sec', 'op')), may hold values from -0.25 to 0.25
- right_ops: float32 [1024, 512, 512], P(('sec', 'op')), may hold values from -0.25 to 0.25
Outputs:
- cheb_last: float32 [32, 512, 512], P('sec', 'op')
- cheb_prev: float32 [32, 512, 512], P('sec', 'op')
Inputs may be any that keep to these rules, and one draw needn't show every extreme that they name: `counts`: every sector has between 256 and 512 live states; some sector has exactly 512 and some exactly 256.
All inputs are finite; a program needn't handle non-finite values.
Results may differ from a plain program's by a relative error of at most 0.0001.
Values sent between devices are 32-bit elements; how exact they have to be, the bound alone decides.
A program may use at most 64 MiB of HBM per device.

v0:
```python
import math
import jax
import jax.numpy as jnp
from jax import lax
from jax.sharding import PartitionSpec as P

STEPS = 3


def per_device(theta, counts, pair_source, pair_target, left_ops, right_ops):
    op_count = lax.axis_size("op")
    op_place = lax.axis_index("op")
    sec_place = lax.axis_index("sec")
    sec_local = theta.shape[0]
    row_count = theta.shape[1]
    order_size = theta.shape[2]
    pairs_local = left_ops.shape[0]
    group_blocks = pair_target.shape[0]
    sectors_all = sec_local * lax.axis_size("sec")
    factor = 0.5 / math.sqrt(group_blocks * pairs_local / sec_local)
    highest = lax.Precision.HIGHEST
    my_source = lax.dynamic_index_in_dim(pair_source, op_place, 0, keepdims=False)
    row_numbers = op_place * row_count + jnp.arange(row_count, dtype=jnp.int32)
    row_alive = row_numbers[None, :] < counts[:, None]
    column_alive = jnp.arange(order_size, dtype=jnp.int32)[None, :] < counts[:, None]
    live_mask = (row_alive[:, :, None] & column_alive[:, None, :]).astype(jnp.float32)
    target_hot = (pair_target[None, :] == jnp.arange(sectors_all, dtype=jnp.int32)[:, None]).astype(
        jnp.float32
    )

    def hamiltonian(iterate):
        gathered = lax.all_gather(iterate, "op", axis=1, tiled=True)
        chosen = lax.dynamic_index_in_dim(gathered, my_source, 0, keepdims=False)
        left_product = jnp.einsum("pmr,rn->pmn", left_ops, chosen, precision=highest)
        block_term = jnp.einsum("pmk,pnk->mn", left_product, right_ops, precision=highest)
        split_rows = block_term.reshape(op_count, row_count, order_size)
        block_rows = lax.all_to_all(split_rows, "op", split_axis=0, concat_axis=0, tiled=True)
        flat_rows = block_rows.reshape(group_blocks, row_count * order_size)
        sector_sums = jnp.dot(
            target_hot, flat_rows, precision=highest, preferred_element_type=jnp.float32
        )
        sector_sums = sector_sums.reshape(sectors_all, row_count, order_size)
        whole_sums = lax.psum(sector_sums, "sec")
        own_sums = lax.dynamic_slice_in_dim(whole_sums, sec_place * sec_local, sec_local, 0)
        return factor * own_sums * live_mask

    previous = theta * live_mask
    current = hamiltonian(previous)
    for step_number in range(STEPS - 1):
        following = 2.0 * hamiltonian(current) - previous
        previous, current = (current, following)
    return (current, previous)


def solution(mesh):
    in_specs = (
        P("sec", "op", None),
        P("sec"),
        P("sec"),
        P("sec"),
        P(("sec", "op"), None, None),
        P(("sec", "op"), None, None),
    )
    out_specs = (P("sec", "op", None), P("sec", "op", None))
    return jax.shard_map(
        per_device, mesh=mesh, in_specs=in_specs, out_specs=out_specs, check_vma=False
    )
```

profile of v0, /device:TPU:1, one launch (start us, length us, event | category | flops | bytes accessed | tf_op | source)
XLA Modules:
  0.0 675.0 jit_solution(8471230393268469698)
XLA Ops:
  7.2 0.7 iota_compare_fusion.1
  8.0 0.7 broadcast_compare_fusion
  8.7 1.7 and_select_fusion.3
  10.5 1.2 dynamic_slice.23
  13.7 50.3 %all-gather.4.cloned.1.call-done = f32[2,512,512]{2,0,1:T(2,128)} async-done(((f32[2,32,512]{2,0,1:T(2,128)}), f32[2,512,512]{2,0,1:T(2,128)}) %all-gather.4.cloned.1.call-update) | async-done | bytes 2097168 | tf_op jit(solution)/shard_map/all_gather | solution.py:32
  63.9 2.5 constant_dynamic-slice_fusion.2
  66.4 1.3 copy.18
  67.8 10.3 %fusion.19 = f32[512,4,512]{2,0,1:T(8,128)S(1)} fusion(f32[4,512,512]{2,1,0:T(8,128)} %param.10, f32[1,512,512]{1,2,0:T(8,128)S(1)} %copy.18), kind=kOutput, calls=%fused_computation.19 | convolution fusion | flops 6442450944 | bytes 9437184 | tf_op jit(solution)/shard_map/pmr,rn->pmn/dot_general | solution.py:34
  78.1 13.9 %fusion.4 = f32[512,512,1]{1,0,2:T(8,128)S(1)} fusion(f32[4,512,512]{2,1,0:T(8,128)S(1)} %copy-done, f32[512,4,512]{2,0,1:T(8,128)S(1)} %fusion.19), kind=kOutput, calls=%fused_computation.4 | convolution fusion | flops 6442450944 | bytes 9437184 | tf_op jit(solution)/shard_map/pmk,pnk->mn/dot_general | solution.py:35
  92.0 19.3 %all_to_all.15 = f32[16,32,512]{2,1,0:T(8,128)S(1)} all-to-all(f32[16,32,512]{2,1,0:T(8,128)S(1)} %bitcast.75), channel_id=1, replica_groups=mesh['sec'=16,'op'=16] {'op'}, dimensions={0} | all-to-all | bytes 2097152 | tf_op jit(solution)/shard_map/all_to_all | solution.py:37
  111.3 2.9 fusion.12
  114.2 115.1 %all-reduce.4.cloned.1.call-done = f32[32,32,512]{2,0,1:T(8,128)} async-done(((f32[32,32,512]{2,0,1:T(8,128)}), f32[32,32,512]{2,0,1:T(8,128)}) %all-reduce.4.cloned.1.call-update) | async-done | bytes 2097168 | tf_op jit(solution)/shard_map/psum | solution.py:43
  229.4 1.8 and_select_fusion.2
  231.3 50.7 %all-gather.6.cloned.1.call-done = f32[2,512,512]{2,0,1:T(2,128)} async-done(((f32[2,32,512]{2,0,1:T(2,128)}), f32[2,512,512]{2,0,1:T(2,128)}) %all-gather.6.cloned.1.call-update) | async-done | bytes 2097168 | tf_op jit(solution)/shard_map/all_gather | solution.py:32
  282.0 2.5 constant_dynamic-slice_fusion.1
  284.5 1.3 copy.21
  285.8 10.3 %fusion.17 = f32[512,4,512]{2,0,1:T(8,128)S(1)} fusion(f32[4,512,512]{2,1,0:T(8,128)} %param.10, f32[1,512,512]{1,2,0:T(8,128)S(1)} %copy.21), kind=kOutput, calls=%fused_computation.17 | convolution fusion | flops 6442450944 | bytes 9437184 | tf_op jit(solution)/shard_map/pmr,rn->pmn/dot_general | solution.py:34
  296.1 13.7 %fusion.2 = f32[512,512,1]{1,0,2:T(8,128)S(1)} fusion(f32[4,512,512]{2,1,0:T(8,128)S(1)} %copy-done.1, f32[512,4,512]{2,0,1:T(8,128)S(1)} %fusion.17), kind=kOutput, calls=%fused_computation.2 | convolution fusion | flops 6442450944 | bytes 9437184 | tf_op jit(solution)/shard_map/pmk,pnk->mn/dot_general | solution.py:35
  309.9 19.4 %all_to_all.16 = f32[16,32,512]{2,1,0:T(8,128)S(1)} all-to-all(f32[16,32,512]{2,1,0:T(8,128)S(1)} %bitcast.76), channel_id=1, replica_groups=mesh['sec'=16,'op'=16] {'op'}, dimensions={0} | all-to-all | bytes 2097152 | tf_op jit(solution)/shard_map/all_to_all | solution.py:37
  329.2 2.9 fusion.9
  332.2 115.3 %all-reduce.6.cloned.1.call-done = f32[32,32,512]{2,0,1:T(8,128)} async-done(((f32[32,32,512]{2,0,1:T(8,128)}), f32[32,32,512]{2,0,1:T(8,128)}) %all-reduce.6.cloned.1.call-update) | async-done | bytes 2097168 | tf_op jit(solution)/shard_map/psum | solution.py:43
  447.5 1.9 fusion.22
  449.5 50.4 %all-gather.8.cloned.1.call-done = f32[2,512,512]{2,0,1:T(2,128)} async-done(((f32[2,32,512]{2,0,1:T(2,128)}), f32[2,512,512]{2,0,1:T(2,128)}) %all-gather.8.cloned.1.call-update) | async-done | bytes 2097168 | tf_op jit(solution)/shard_map/all_gather | solution.py:32
  500.0 2.5 constant_dynamic-slice_fusion
  502.5 1.3 copy.24
  503.8 10.3 %fusion.15 = f32[512,4,512]{2,0,1:T(8,128)S(1)} fusion(f32[4,512,512]{2,1,0:T(8,128)} %param.10, f32[1,512,512]{1,2,0:T(8,128)S(1)} %copy.24), kind=kOutput, calls=%fused_computation.15 | convolution fusion | flops 6442450944 | bytes 9437184 | tf_op jit(solution)/shard_map/pmr,rn->pmn/dot_general | solution.py:34
  514.1 13.8 %fusion = f32[512,512,1]{1,0,2:T(8,128)S(1)} fusion(f32[4,512,512]{2,1,0:T(8,128)S(1)} %copy-done.2, f32[512,4,512]{2,0,1:T(8,128)S(1)} %fusion.15), kind=kOutput, calls=%fused_computation | convolution fusion | flops 6442450944 | bytes 9437184 | tf_op jit(solution)/shard_map/pmk,pnk->mn/dot_general | solution.py:35
  528.0 19.4 %all_to_all.17 = f32[16,32,512]{2,1,0:T(8,128)S(1)} all-to-all(f32[16,32,512]{2,1,0:T(8,128)S(1)} %bitcast.77), channel_id=1, replica_groups=mesh['sec'=16,'op'=16] {'op'}, dimensions={0} | all-to-all | bytes 2097152 | tf_op jit(solution)/shard_map/all_to_all | solution.py:37
  547.4 2.9 fusion.6
  550.3 0.7 copy.28
  551.0 114.5 %all-reduce.8.cloned.1.call-done = f32[32,32,512]{2,0,1:T(8,128)} async-done(((f32[32,32,512]{2,0,1:T(8,128)}), f32[32,32,512]{2,0,1:T(8,128)}) %all-reduce.8.cloned.1.call-update) | async-done | bytes 2097168 | tf_op jit(solution)/shard_map/psum | solution.py:43
  665.5 1.4 fusion.24
  (26 shorter events, 1.1 us)
Async XLA Ops:
  7.2 56.8 %all-gather.4.cloned.1.call-start = ((), (), s32[]{:S(2)}) async-start(), calls=%async_computation.3 | async-start | bytes 2228224 | tf_op jit(solution)/shard_map/all_gather | solution.py:32
  10.4 219.0 %all-reduce.4.cloned.1.call-start = ((), (), s32[]{:S(2)}) async-start(), calls=%async_computation.4 | async-start | bytes 4194304 | tf_op jit(solution)/shard_map/psum | solution.py:43
  67.8 10.3 %copy-start = (f32[4,512,512]{2,1,0:T(8,128)S(1)}, f32[4,512,512]{2,1,0:T(8,128)}, u32[]{:S(2)}) copy-start(f32[4,512,512]{2,1,0:T(8,128)} %param.11) | copy-start | bytes 12582916
  78.1 33.2 %copy-start.5 = (s32[16]{0:T(128)S(1)}, s32[16]{0:T(128)}, u32[]{:S(2)}) copy-start(s32[16]{0:T(128)} %param.9) | copy-start | bytes 196
  114.2 167.8 %all-gather.6.cloned.1.call-start = ((), (), s32[]{:S(2)}) async-start(), calls=%async_computation.5 | async-start | bytes 2228224 | tf_op jit(solution)/shard_map/all_gather | solution.py:32
  231.3 216.3 %all-reduce.6.cloned.1.call-start = ((), (), s32[]{:S(2)}) async-start(), calls=%async_computation.6 | async-start | bytes 4194304 | tf_op jit(solution)/shard_map/psum | solution.py:43
  285.8 10.3 %copy-start.1 = (f32[4,512,512]{2,1,0:T(8,128)S(1)}, f32[4,512,512]{2,1,0:T(8,128)}, u32[]{:S(2)}) copy-start(f32[4,512,512]{2,1,0:T(8,128)} %param.11) | copy-start | bytes 12582916
  309.8 137.7 %copy-start.4 = (f32[2,32,512]{2,1,0:T(8,128)S(1)}, f32[2,32,512]{2,1,0:T(8,128)}, u32[]{:S(2)}) copy-start(f32[2,32,512]{2,1,0:T(8,128)} %param.6) | copy-start | bytes 393220
  332.2 167.8 %all-gather.8.cloned.1.call-start = ((), (), s32[]{:S(2)}) async-start(), calls=%async_computation.7 | async-start | bytes 2228224 | tf_op jit(solution)/shard_map/all_gather | solution.py:32
  449.5 216.0 %all-reduce.8.cloned.1.call-start = ((), (), s32[]{:S(2)}) async-start(), calls=%async_computation.8 | async-start | bytes 4194304 | tf_op jit(solution)/shard_map/psum | solution.py:43
  503.8 10.4 %copy-start.2 = (f32[4,512,512]{2,1,0:T(8,128)S(1)}, f32[4,512,512]{2,1,0:T(8,128)}, u32[]{:S(2)}) copy-start(f32[4,512,512]{2,1,0:T(8,128)} %param.11) | copy-start | bytes 12582916
  528.0 22.3 %copy-start.3 = (f32[2,32,512]{2,0,1:T(2,128)S(1)}, f32[2,32,512]{2,0,1:T(2,128)}, u32[]{:S(2)}) copy-start(f32[2,32,512]{2,0,1:T(2,128)} %fusion.22) | copy-start | bytes 393220
Sparse Core Ops, SparseCore 0:
  11.0 52.8 all-gather.3
  114.3 115.0 all-reduce.3
  232.4 49.5 all-gather.5
  332.3 115.2 all-reduce.5
  450.4 49.5 all-gather.7
  550.4 115.0 all-reduce.7
where the time goes:
time: 680 us; the launch traced here: 675 us
  waiting for transfers between devices  496 us (73%)
  matrix products  81 us (12%)
  blocking collectives  58 us (9%)
  between operations  16.7 us (2%)
  local copies, waits for them, and re-layouts  14 us (2%)
  other arithmetic  8.39 us (1%)
    psum x3, waiting for transfers between devices, hamiltonian(): whole_sums = lax.psum(sector_sums, 'sec')  345 us
    all_gather x3, waiting for transfers between devices, hamiltonian(): gathered = lax.all_gather(iterate, 'op', axis=1, tiled=True)  151 us
    all_to_all x3, blocking collectives, hamiltonian(): lax.all_to_all(split_rows, 'op', split_axis=0, concat_axis=0, tiled=True)  58 us
    dot_general x3, matrix products, hamiltonian(): jnp.einsum('pmk,pnk->mn', left_product, right_ops, precision=highest)  41.5 us
    dot_general x3, matrix products, hamiltonian(): jnp.einsum('pmr,rn->pmn', left_ops, chosen, precision=highest)  30.9 us
  transfers between devices with their start and end apart: 6, of which 6 were waited for; matrix products, arithmetic and copies ran while one was open for 0% of the time, Pallas kernels for 0%

commit v1 on v0

--- a/solution.py
+++ b/solution.py
@@ -40,7 +40,8 @@
             target_hot, flat_rows, precision=highest, preferred_element_type=jnp.float32
         )
         sector_sums = sector_sums.reshape(sectors_all, row_count, order_size)
-        whole_sums = lax.psum(sector_sums, "sec")
+        shards = lax.all_gather(sector_sums, "sec")
+        whole_sums = jnp.sum(shards, axis=0)
         own_sums = lax.dynamic_slice_in_dim(whole_sums, sec_place * sec_local, sec_local, 0)
         return factor * own_sums * live_mask
 

time: 680 us -> 890 us (1.31)
  waiting for transfers between devices: 496 us -> 670 us
  other arithmetic: 8.39 us -> 44.4 us
    all_gather x0 -> x3, waiting for transfers between devices: none -> 526 us  [hamiltonian(): shards = lax.all_gather(sector_sums, 'sec')]
    psum x3 -> x0, waiting for transfers between devices: 345 us -> none  [hamiltonian(): whole_sums = lax.psum(sector_sums, 'sec')]
    reduce_sum x0 -> x3, other arithmetic: none -> 38.1 us  [hamiltonian(): whole_sums = jnp.sum(shards, axis=0)]
where the time goes in v1:
time: 890 us; the launch traced here: 885 us
  waiting for transfers between devices  670 us (75%)
  matrix products  81.3 us (9%)
  blocking collectives  57.9 us (7%)
  other arithmetic  44.4 us (5%)
  between operations  16.5 us (2%)
  local copies, waits for them, and re-layouts  14.4 us (2%)
    all_gather x3, waiting for transfers between devices, hamiltonian(): shards = lax.all_gather(sector_sums, 'sec')  526 us
    all_gather x3, waiting for transfers between devices, hamiltonian(): gathered = lax.all_gather(iterate, 'op', axis=1, tiled=True)  145 us
    all_to_all x3, blocking collectives, hamiltonian(): lax.all_to_all(split_rows, 'op', split_axis=0, concat_axis=0, tiled=True)  57.9 us
    dot_general x3, matrix products, hamiltonian(): jnp.einsum('pmk,pnk->mn', left_product, right_ops, precision=highest)  41.5 us
    reduce_sum x3, other arithmetic, hamiltonian(): whole_sums = jnp.sum(shards, axis=0)  38.1 us
    dot_general x3, matrix products, hamiltonian(): jnp.einsum('pmr,rn->pmn', left_ops, chosen, precision=highest)  31.1 us
  transfers between devices with their start and end apart: 6, of which 6 were waited for; matrix products, arithmetic and copies ran while one was open for 0% of the time, Pallas kernels for 0%

profile of v1, /device:TPU:1, one launch (start us, length us, event | category | flops | bytes accessed | tf_op | source)
XLA Modules:
  0.0 885.1 jit_solution(8894595678948539102)
XLA Ops:
  8.7 1.7 and_select_fusion.3
  10.5 1.2 dynamic_slice.23
  13.7 50.3 %all-gather.10.cloned.1.call-done = f32[2,512,512]{2,0,1:T(2,128)} async-done(((f32[2,32,512]{2,0,1:T(2,128)}), f32[2,512,512]{2,0,1:T(2,128)}) %all-gather.10.cloned.1.call-update) | async-done | bytes 2097168 | tf_op jit(solution)/shard_map/all_gather | solution.py:32
  63.9 2.5 constant_dynamic-slice_fusion.2
  66.4 1.3 copy.24
  67.8 10.4 %fusion.19 = f32[512,4,512]{2,0,1:T(8,128)S(1)} fusion(f32[4,512,512]{2,1,0:T(8,128)} %param.10, f32[1,512,512]{1,2,0:T(8,128)S(1)} %copy.24), kind=kOutput, calls=%fused_computation.19 | convolution fusion | flops 6442450944 | bytes 9437184 | tf_op jit(solution)/shard_map/pmr,rn->pmn/dot_general | solution.py:34
  78.2 14.1 %fusion.4 = f32[512,512,1]{1,0,2:T(8,128)S(1)} fusion(f32[4,512,512]{2,1,0:T(8,128)S(1)} %copy-done, f32[512,4,512]{2,0,1:T(8,128)S(1)} %fusion.19), kind=kOutput, calls=%fused_computation.4 | convolution fusion | flops 6442450944 | bytes 9437184 | tf_op jit(solution)/shard_map/pmk,pnk->mn/dot_general | solution.py:35
  92.2 19.3 %all_to_all.15 = f32[16,32,512]{2,1,0:T(8,128)S(1)} all-to-all(f32[16,32,512]{2,1,0:T(8,128)S(1)} %bitcast.83), channel_id=1, replica_groups=mesh['sec'=16,'op'=16] {'op'}, dimensions={0} | all-to-all | bytes 2097152 | tf_op jit(solution)/shard_map/all_to_all | solution.py:37
  111.5 2.9 fusion.12
  114.4 175.4 %all-gather.16.cloned.1.call-done = f32[512,32,512]{2,0,1:T(8,128)} async-done(((f32[32,32,512]{2,0,1:T(8,128)}), f32[512,32,512]{2,0,1:T(8,128)}) %all-gather.16.cloned.1.call-update) | async-done | bytes 33554448 | tf_op jit(solution)/shard_map/all_gather | solution.py:43
  289.9 12.7 %reduce_sum.27 = f32[32,32,512]{2,0,1:T(8,128)S(1)} reduce(f32[16,32,32,512]{3,1,0,2:T(8,128)} %bitcast.80, f32[]{:T(128)} %constant.29.clone.1), dimensions={0}, to_apply=%region_0.1 | reduce | flops 7864320 | bytes 35651588 | tf_op jit(solution)/shard_map/reduce_sum | solution.py:44
  302.6 1.0 and_select_fusion.2
  303.9 47.0 %all-gather.12.cloned.1.call-done = f32[2,512,512]{2,0,1:T(2,128)} async-done(((f32[2,32,512]{2,0,1:T(2,128)}), f32[2,512,512]{2,0,1:T(2,128)}) %all-gather.12.cloned.1.call-update) | async-done | bytes 2097168 | tf_op jit(solution)/shard_map/all_gather | solution.py:32
  351.0 2.5 constant_dynamic-slice_fusion.1
  353.5 1.3 copy.27
  354.8 10.3 %fusion.17 = f32[512,4,512]{2,0,1:T(8,128)S(1)} fusion(f32[4,512,512]{2,1,0:T(8,128)} %param.10, f32[1,512,512]{1,2,0:T(8,128)S(1)} %copy.27), kind=kOutput, calls=%fused_computation.17 | convolution fusion | flops 6442450944 | bytes 9437184 | tf_op jit(solution)/shard_map/pmr,rn->pmn/dot_general | solution.py:34
  365.1 13.7 %fusion.2 = f32[512,512,1]{1,0,2:T(8,128)S(1)} fusion(f32[4,512,512]{2,1,0:T(8,128)S(1)} %copy-done.1, f32[512,4,512]{2,0,1:T(8,128)S(1)} %fusion.17), kind=kOutput, calls=%fused_computation.2 | convolution fusion | flops 6442450944 | bytes 9437184 | tf_op jit(solution)/shard_map/pmk,pnk->mn/dot_general | solution.py:35
  378.8 19.3 %all_to_all.16 = f32[16,32,512]{2,1,0:T(8,128)S(1)} all-to-all(f32[16,32,512]{2,1,0:T(8,128)S(1)} %bitcast.84), channel_id=1, replica_groups=mesh['sec'=16,'op'=16] {'op'}, dimensions={0} | all-to-all | bytes 2097152 | tf_op jit(solution)/shard_map/all_to_all | solution.py:37
  398.1 2.9 fusion.9
  401.1 175.4 %all-gather.18.cloned.1.call-done = f32[512,32,512]{2,0,1:T(8,128)} async-done(((f32[32,32,512]{2,0,1:T(8,128)}), f32[512,32,512]{2,0,1:T(8,128)}) %all-gather.18.cloned.1.call-update) | async-done | bytes 33554448 | tf_op jit(solution)/shard_map/all_gather | solution.py:43
  576.5 12.7 %reduce_sum.28 = f32[32,32,512]{2,0,1:T(8,128)S(1)} reduce(f32[16,32,32,512]{3,1,0,2:T(8,128)} %bitcast.82, f32[]{:T(128)} %constant.29.clone.1), dimensions={0}, to_apply=%region_1.2 | reduce | flops 7864320 | bytes 35651588 | tf_op jit(solution)/shard_map/reduce_sum | solution.py:44
  589.2 0.9 fusion.22
  590.2 47.3 %all-gather.14.cloned.1.call-done = f32[2,512,512]{2,0,1:T(2,128)} async-done(((f32[2,32,512]{2,0,1:T(2,128)}), f32[2,512,512]{2,0,1:T(2,128)}) %all-gather.14.cloned.1.call-update) | async-done | bytes 2097168 | tf_op jit(solution)/shard_map/all_gather | solution.py:32
  637.5 2.5 constant_dynamic-slice_fusion
  640.0 1.3 copy.30
  641.3 10.5 %fusion.15 = f32[512,4,512]{2,0,1:T(8,128)S(1)} fusion(f32[4,512,512]{2,1,0:T(8,128)} %param.10, f32[1,512,512]{1,2,0:T(8,128)S(1)} %copy.30), kind=kOutput, calls=%fused_computation.15 | convolution fusion | flops 6442450944 | bytes 9437184 | tf_op jit(solution)/shard_map/pmr,rn->pmn/dot_general | solution.py:34
  651.8 13.7 %fusion = f32[512,512,1]{1,0,2:T(8,128)S(1)} fusion(f32[4,512,512]{2,1,0:T(8,128)S(1)} %copy-done.2, f32[512,4,512]{2,0,1:T(8,128)S(1)} %fusion.15), kind=kOutput, calls=%fused_computation | convolution fusion | flops 6442450944 | bytes 9437184 | tf_op jit(solution)/shard_map/pmk,pnk->mn/dot_general | solution.py:35
  665.6 19.4 %all_to_all.17 = f32[16,32,512]{2,1,0:T(8,128)S(1)} all-to-all(f32[16,32,512]{2,1,0:T(8,128)S(1)} %bitcast.85), channel_id=1, replica_groups=mesh['sec'=16,'op'=16] {'op'}, dimensions={0} | all-to-all | bytes 2097152 | tf_op jit(solution)/shard_map/all_to_all | solution.py:37
  685.0 2.9 fusion.6
  688.6 174.8 %all-gather.20.cloned.1.call-done = f32[512,32,512]{2,0,1:T(8,128)} async-done(((f32[32,32,512]{2,0,1:T(8,128)}), f32[512,32,512]{2,0,1:T(8,128)}) %all-gather.20.cloned.1.call-update) | async-done | bytes 33554448 | tf_op jit(solution)/shard_map/all_gather | solution.py:43
  863.4 12.7 %reduce_sum.29 = f32[32,32,512]{2,0,1:T(8,128)S(1)} reduce(f32[16,32,32,512]{3,1,0,2:T(8,128)} %bitcast.81, f32[]{:T(128)} %constant.29.clone.1), dimensions={0}, to_apply=%region_2.3 | reduce | flops 7864320 | bytes 35651588 | tf_op jit(solution)/shard_map/reduce_sum | solution.py:44
  876.1 1.3 fusion.24
  (31 shorter events, 3.5 us)
Async XLA Ops:
  7.2 56.8 %all-gather.10.cloned.1.call-start = ((), (), s32[]{:S(2)}) async-start(), calls=%async_computation.3 | async-start | bytes 2228224 | tf_op jit(solution)/shard_map/all_gather | solution.py:32
  10.4 279.4 %all-gather.16.cloned.1.call-start = ((), (), s32[]{:S(2)}) async-start(), calls=%async_computation.6 | async-start | bytes 35651584 | tf_op jit(solution)/shard_map/all_gather | solution.py:43
  67.8 10.4 %copy-start = (f32[4,512,512]{2,1,0:T(8,128)S(1)}, f32[4,512,512]{2,1,0:T(8,128)}, u32[]{:S(2)}) copy-start(f32[4,512,512]{2,1,0:T(8,128)} %param.11) | copy-start | bytes 12582916
  78.2 33.3 %copy-start.6 = (s32[16]{0:T(128)S(1)}, s32[16]{0:T(128)}, u32[]{:S(2)}) copy-start(s32[16]{0:T(128)} %param.9) | copy-start | bytes 196
  114.4 236.6 %all-gather.12.cloned.1.call-start = ((), (), s32[]{:S(2)}) async-start(), calls=%async_computation.4 | async-start | bytes 2228224 | tf_op jit(solution)/shard_map/all_gather | solution.py:32
  302.6 1.4 copy-start.3
  303.6 272.9 %all-gather.18.cloned.1.call-start = ((), (), s32[]{:S(2)}) async-start(), calls=%async_computation.7 | async-start | bytes 35651584 | tf_op jit(solution)/shard_map/all_gather | solution.py:43
  354.8 10.3 %copy-start.1 = (f32[4,512,512]{2,1,0:T(8,128)S(1)}, f32[4,512,512]{2,1,0:T(8,128)}, u32[]{:S(2)}) copy-start(f32[4,512,512]{2,1,0:T(8,128)} %param.11) | copy-start | bytes 12582916
  401.0 236.5 %all-gather.14.cloned.1.call-start = ((), (), s32[]{:S(2)}) async-start(), calls=%async_computation.5 | async-start | bytes 2228224 | tf_op jit(solution)/shard_map/all_gather | solution.py:32
  576.5 12.7 %copy-start.5 = (f32[2,32,512]{2,1,0:T(8,128)S(1)}, f32[2,32,512]{2,1,0:T(8,128)}, u32[]{:S(2)}) copy-start(f32[2,32,512]{2,1,0:T(8,128)} %param.6) | copy-start | bytes 393220
  590.1 273.3 %all-gather.20.cloned.1.call-start = ((), (), s32[]{:S(2)}) async-start(), calls=%async_computation.8 | async-start | bytes 35651584 | tf_op jit(solution)/shard_map/all_gather | solution.py:43
  641.3 10.5 %copy-start.2 = (f32[4,512,512]{2,1,0:T(8,128)S(1)}, f32[4,512,512]{2,1,0:T(8,128)}, u32[]{:S(2)}) copy-start(f32[4,512,512]{2,1,0:T(8,128)} %param.11) | copy-start | bytes 12582916
  665.6 22.4 %copy-start.4 = (f32[2,32,512]{2,0,1:T(2,128)S(1)}, f32[2,32,512]{2,0,1:T(2,128)}, u32[]{:S(2)}) copy-start(f32[2,32,512]{2,0,1:T(2,128)} %fusion.22) | copy-start | bytes 393220
Sparse Core Ops, SparseCore 0:
  11.0 52.8 all-gather.9
  114.5 175.3 all-gather.15
  303.7 47.2 all-gather.11
  401.1 175.3 all-gather.17
  590.3 47.2 all-gather.13
  688.0 175.3 all-gather.19
